TPU v7x, 256 devices: a whole 4x4x8 slice. The times are simulated.
256 devices in a mesh: lev: 4 (over y_lo, core), tile: 64 (over x, y_hi, z).
Axes of the slice: x: 4, y: 4 (y_hi: 2, y_lo: 2; y = y_hi * 2 + y_lo), z: 8, core: 2. Of those that a mesh axis runs over, the one named last changes fastest.
Arguments:
- control: float32 [96, 64, 256], P(None, 'tile'), may hold values from -6 to 6
- emit_mask: int32 [64, 256], P('tile'), may hold values 0 or 1
- bin_profile: float32 [96], replicated, may hold values from 0.2 to 2
- plume_profile: float32 [64], P('lev'), may hold values from 0.2 to 2
- courant: float32 [2, 64, 64, 256], P(None, 'lev', 'tile'), may hold values from 0.05 to 0.24
- upwind: int32 [2, 64, 64, 256], P(None, 'lev', 'tile'), may hold values from 0 to 1
- bin_speed: float32 [96], replicated, may hold values from 0.2 to 1000
- level_factor: float32 [64], replicated, may hold values from 0.4 to 1.6
- background: float32 [96, 64, 64, 256], P(None, 'lev', 'tile'), may hold values from 0.1 to 1
- coag_rate: float32 [64, 64, 256], P('lev', 'tile'), may hold values from 0.002 to 0.01
- obs_weight: float32 [96], replicated, may hold values from 0.2 to 2
- obs_precision: float32 [64, 256], P('tile'), may hold values from 0.5 to 2
Outputs:
- obs_tangent: float32 [64, 256], P('tile')
- hess_vec: float32 [96, 64, 256], P(None, 'tile')
Inputs may be any that keep to these rules, and one draw needn't show every extreme that they name: `emit_mask`: 1 marks an emitting column.
All inputs are finite; a program needn't handle non-finite values. No bound on the sum of `emit_mask` on one device may be relied on, other than what follows from the above.
Results may differ from a plain program's by a relative error of at most 0.0003.
Values sent between devices are 32-bit elements; how exact they have to be, the bound alone decides.
A program may use at most 64 MiB of HBM per device.

v0:
```python
import functools

import jax
import jax.numpy as jnp
from jax import lax
from jax.experimental import pallas as pl
from jax.experimental.pallas import tpu as pltpu
from jax.sharding import PartitionSpec as P

MESH = pl.DeviceIdType.MESH
F32, BF16 = jnp.float32, jnp.bfloat16


def split(value):
    high = value.astype(BF16)
    return high, (value - high.astype(F32)).astype(BF16)


def dot3(a, b):
    a_hi, a_lo = split(a)
    b_hi, b_lo = split(b)
    dot = functools.partial(jnp.dot, preferred_element_type=F32)
    return dot(a_hi, b_hi) + (dot(a_hi, b_lo) + dot(a_lo, b_hi))


def iota(shape, dim):
    return lax.broadcasted_iota(jnp.int32, shape, dim)


def pad_row(row, lanes):
    return jnp.concatenate([row, jnp.zeros((1, lanes - row.shape[1]), row.dtype)], axis=1)


def column(row, rows):
    shape = (rows, row.shape[1])
    picked = jnp.where(iota(shape, 0) == iota(shape, 1), jnp.broadcast_to(row, shape), 0.0)
    return jnp.sum(picked, axis=1, keepdims=True)


def kernel(
    nb, nl, total, scale,
    control, mask_in, profile_in, plume_in, courant, upwind, speed_in, factor_in, background, rate_in, weight_in, prec_in,
    obs_out, hess_out,
    bg, ctl, mask, profile, plume, cour, upw, speed, factor, rate, weight, prec,
    lhs, amp, rb, gb, bfield, face, nface, coef, ncoef, quot, nquot, masked, edge, kern,
    du_in, self_in, left_in, right_in, t_lev, t_left, t_right, t_own, s_own, out_buf,
    load_sem, bg_sem,
    halo_send, halo_recv, down_send, down_recv, edge_send, edge_recv,
    du_send, du_recv, self_send, self_recv, left_send, left_recv, right_send, right_recv,
    tl_send, tl_recv, tx_send, tx_recv, ag_send, ag_recv,
):
    lev, tile = lax.axis_index("lev"), lax.axis_index("tile")
    tiles = lax.axis_size("tile")
    before, after = lax.rem(tile + tiles - 1, tiles), lax.rem(tile + 1, tiles)
    ny = bg.shape[2]
    chunk = nb // 4

    def at(lev_to, tile_to):
        return {"lev": lev_to, "tile": tile_to}

    def send(src, dst, send_sem, recv_sem, lev_to, tile_to):
        return pltpu.make_async_remote_copy(
            src_ref=src, dst_ref=dst, send_sem=send_sem, recv_sem=recv_sem,
            device_id=at(lev_to, tile_to), device_id_type=MESH,
        )

    def arrived(dst, sem):
        pltpu.make_async_copy(dst, dst, sem).wait()

    small = [
        (courant.at[:, :, 0, :], cour), (upwind.at[:, :, 0, :], upw), (plume_in, plume), (control.at[:, 0, :], ctl),
        (mask_in, mask), (speed_in, speed), (factor_in, factor), (weight_in, weight), (profile_in, profile),
        (rate_in.at[:, 0, :], rate), (prec_in, prec),
    ]
    loads = [pltpu.make_async_copy(a, b, load_sem.at[n]) for n, (a, b) in enumerate(small)]
    for copy in loads:
        copy.start()

    def bg_copy(l):
        return pltpu.make_async_copy(background.at[:, l, 0, :], bg.at[l], bg_sem.at[l])

    def bg_start(l, _):
        bg_copy(l).start()
        return 0

    lax.fori_loop(0, nl, bg_start, 0)

    barrier = pltpu.get_barrier_semaphore()
    for k in range(1, 4):
        pl.semaphore_signal(barrier, inc=1, device_id=at(lev ^ k, tile), device_id_type=MESH)
    for near in (before, after):
        for k in range(4):
            pl.semaphore_signal(barrier, inc=1, device_id=at(k, near), device_id_type=MESH)

    for n in range(3):
        loads[n].wait()
    plume_col = column(plume[...], nl)
    scaled = jnp.where(upw[...] == 1, cour[...], -cour[...]) * plume_col[None]
    face[0, 0:nl, :] = scaled[0]
    face[1, 0:nl, :] = scaled[1]
    face[2, 0:nl, :] = jnp.broadcast_to(plume_col, (nl, ny))
    for k in range(1, 4):
        @pl.when(lev + k > 3)
        def _():
            face[:, k * nl:(k + 1) * nl, :] = jnp.zeros((3, nl, ny), F32)
            nface[k * nl:(k + 1) * nl, :] = jnp.zeros((nl, ny), F32)
    for n in range(3, 5):
        loads[n].wait()
    masked[0] = ctl[...] * mask[...].astype(F32)

    pl.semaphore_wait(barrier, 11)

    def halo(k):
        return send(face.at[0, pl.ds(0, nl)], nface.at[pl.ds(k * nl, nl)], halo_send.at[k], halo_recv.at[k], lev - k, before)

    def down(k):
        return send(face.at[:, pl.ds(0, nl)], face.at[:, pl.ds(k * nl, nl)], down_send.at[k], down_recv.at[k], lev - k, tile)

    edges = [
        send(masked.at[0], edge.at[0], edge_send.at[0], edge_recv.at[0], lev, after),
        send(masked.at[0], edge.at[1], edge_send.at[1], edge_recv.at[1], lev, before),
    ]
    halo(0).start()
    for k in range(1, 4):
        @pl.when(lev >= k)
        def _():
            halo(k).start()
    for copy in edges:
        copy.start()
    for k in range(1, 4):
        @pl.when(lev >= k)
        def _():
            down(k).start()

    for n in range(5, 11):
        loads[n].wait()
    row_i, lane_i = iota((nb, 128), 0), iota((nb, 128), 1)
    weight_row = pad_row(weight[...], 128)
    weight_col = column(weight_row, nb)
    shifted = jnp.broadcast_to(weight_row, (nb, 128))
    for bit in range(7):
        shifted = jnp.where((row_i >> bit) & 1 == 1, pltpu.roll(shifted, 128 - (1 << bit), 1), shifted)
    mixing = jnp.where(row_i + lane_i < nb, shifted, 0.0) - weight_row - weight_col
    mix_hi, mix_lo = split(jnp.where(lane_i < nb, mixing, 0.0))
    lhs[0:nb, 0:128] = mix_hi
    lhs[0:nb, 128:256] = mix_hi
    lhs[nb:2 * nb, 0:128] = mix_lo
    lhs[nb:2 * nb, 128:256] = jnp.zeros((nb, 128), BF16)

    speed_col = column(pad_row(speed[...], 128), nb)
    profile_col = column(pad_row(profile[...], 128), nb)
    here = pltpu.roll(jnp.broadcast_to(pad_row(factor[...], 128), (8, 128)), lax.rem(128 - lev * nl, 128), 1)[0:1]
    fall = speed_col * jnp.where(iota((1, 128), 1) < total, here, 0.0)
    inverse = 1.0 / (1.0 + fall)
    gain = fall * inverse
    for l in range(nl):
        rb[l] = jnp.broadcast_to(inverse[:, l:l + 1], (nb, 128))
        gb[l] = jnp.broadcast_to(gain[:, l:l + 1], (nb, 128))
    chain = jnp.where(lane_i < nl, 1.0, gain)
    step = 1
    while step < total:
        chain = chain * jnp.where(lane_i >= step, pltpu.roll(chain, step, 1), 1.0)
        step *= 2
    chain = jnp.where(lane_i < nl, 0.0, chain)[:, 0:total]

    masked[1] = pltpu.roll(masked[0], 1, 1)
    masked[2] = pltpu.roll(masked[0], ny - 1, 1)

    def mix_level(l, _):
        bg_copy(l).wait()
        hi, lo = split(bg[l])
        rest = jnp.zeros((128 - nb, ny), BF16)
        both = jnp.dot(lhs[...], jnp.concatenate([hi, rest, lo, rest], axis=0), preferred_element_type=F32)
        amp[l] = weight_col + rate[pl.ds(l, 1), :] * (both[0:nb] + both[nb:2 * nb])
        return 0

    lax.fori_loop(0, nl, mix_level, 0)

    for k in range(1, 4):
        @pl.when(lev + k <= 3)
        def _():
            arrived(face.at[:, pl.ds(k * nl, nl)], down_recv.at[k])
    face_x, face_y = face[0], face[1]
    next_y = pltpu.roll(face_y, ny - 1, 1)
    coef[0] = jnp.maximum(face_y, 0.0)
    coef[1] = -jnp.minimum(next_y, 0.0)
    coef[2] = jnp.maximum(face_x, 0.0)
    coef[3] = face[2] + jnp.minimum(face_x, 0.0) + jnp.minimum(face_y, 0.0) - jnp.maximum(next_y, 0.0)
    for n in range(4):
        quot[n] = dot3(chain, coef[n])

    def rows_of(c):
        return pl.ds(pl.multiple_of(c * chunk, 8), chunk)

    def wide(value):
        return jnp.concatenate([value] * (ny // 128), axis=1)

    def du(i, c):
        return send(kern.at[c, pl.ds(0, 2)], du_in.at[lev], du_send.at[i], du_recv.at[lev], c, tile)

    def self_(i, c):
        return send(kern.at[c, 3], self_in.at[lev], self_send.at[i], self_recv.at[lev], c, tile)

    def left(c):
        return send(kern.at[c, 2], left_in.at[lev], left_send.at[c], left_recv.at[lev], c, before)

    def right(c):
        return send(kern.at[c, 4], right_in.at[lev], right_send.at[c], right_recv.at[lev], c, after)

    profile_wide = jnp.broadcast_to(profile_col, (nb, 128))
    rb[nl] = profile_wide

    def settle(i, _):
        c = lax.rem(lev + 1 + i, 4)
        rows = rows_of(c)
        value = jnp.zeros((chunk, ny), F32)
        sums = [jnp.zeros((chunk, ny), F32) for _ in range(4)]
        for l in range(nl):
            value = amp[l, rows, :] * wide(rb[l, rows, :]) + value * wide(gb[l, rows, :])
            bfield[l, rows, :] = value
            for n in range(4):
                sums[n] = sums[n] + value * coef[n, l:l + 1, :]
        prof = wide(rb[nl, rows, :])
        for n in range(4):
            kern[c, n] = prof * (sums[n] + value * quot[n, rows, :])

        @pl.when(i < 3)
        def _():
            du(i, c).start()
        left(c).start()
        return 0

    lax.fori_loop(0, 4, settle, 0)

    arrived(nface.at[pl.ds(0, nl)], halo_recv.at[0])
    for k in range(1, 4):
        @pl.when(lev + k <= 3)
        def _():
            arrived(nface.at[pl.ds(k * nl, nl)], halo_recv.at[k])
    ncoef[0] = jnp.maximum(nface[...], 0.0)
    ncoef[1] = -jnp.minimum(nface[...], 0.0)
    for n in range(2):
        nquot[n] = dot3(chain, ncoef[n])
    for n in range(2):
        arrived(edge.at[n], edge_recv.at[n])

    def finish(i, t_sum):
        c = lax.rem(lev + 1 + i, 4)
        rows = rows_of(c)
        sums = [jnp.zeros((chunk, ny), F32) for _ in range(2)]
        for l in range(nl):
            value = bfield[l, rows, :]
            for n in range(2):
                sums[n] = sums[n] + value * ncoef[n, l:l + 1, :]
        prof = wide(rb[nl, rows, :])
        value = bfield[nl - 1, rows, :]
        k_self = kern[c, 3] - prof * (sums[0] + value * nquot[0, rows, :])
        k_right = prof * (sums[1] + value * nquot[1, rows, :])
        kern[c, 3] = k_self
        kern[c, 4] = k_right

        @pl.when(i < 3)
        def _():
            self_(i, c).start()
        right(c).start()
        part = (
            masked[0, rows, :] * k_self + edge[0, rows, :] * kern[c, 2] + edge[1, rows, :] * k_right
            + masked[1, rows, :] * kern[c, 0] + masked[2, rows, :] * kern[c, 1]
        )
        for r in range(0, chunk, 8):
            t_sum = t_sum + part[r:r + 8]
        return t_sum

    t_sum = lax.fori_loop(0, 4, finish, jnp.zeros((8, ny), F32))
    t_mine = jnp.sum(t_sum, axis=0, keepdims=True) * scale
    s_mine = t_mine * prec[...] * scale
    t_own[...] = t_mine
    s_own[...] = s_mine

    t_sends = []
    for k in range(4):
        t_sends.append(send(s_own, t_left.at[lev], tx_send.at[k], tx_recv.at[lev], k, after))
        t_sends.append(send(s_own, t_right.at[lev], tx_send.at[4 + k], tx_recv.at[4 + lev], k, before))
    for k in range(1, 4):
        t_sends.append(send(t_own, t_lev.at[k], tl_send.at[k], tl_recv.at[k], lev ^ k, tile))
    for copy in t_sends:
        copy.start()

    totals = [kern[lev, 0], kern[lev, 1], kern[lev, 3]]
    for k in range(1, 4):
        d = lax.rem(lev + k, 4)
        arrived(du_in.at[d], du_recv.at[d])
        totals[0] = totals[0] + du_in[d, 0]
        totals[1] = totals[1] + du_in[d, 1]
    for k in range(1, 4):
        d = lax.rem(lev + k, 4)
        arrived(self_in.at[d], self_recv.at[d])
        totals[2] = totals[2] + self_in[d]
    t_all = t_mine
    for k in range(1, 4):
        arrived(t_lev.at[k], tl_recv.at[k])
        t_all = t_all + t_lev[k]
    obs_out[...] = t_all
    s_here = t_all * prec[...] * scale
    result = totals[2] * s_here + pltpu.roll(totals[0] * s_here, ny - 1, 1) + pltpu.roll(totals[1] * s_here, 1, 1)
    for k in range(4):
        arrived(left_in.at[k], left_recv.at[k])
        arrived(right_in.at[k], right_recv.at[k])
    from_after = (left_in[0] + left_in[1]) + (left_in[2] + left_in[3])
    from_before = (right_in[0] + right_in[1]) + (right_in[2] + right_in[3])
    for k in range(4):
        arrived(t_left.at[k], tx_recv.at[k])
        arrived(t_right.at[k], tx_recv.at[4 + k])
    s_before = (t_left[0] + t_left[1]) + (t_left[2] + t_left[3])
    s_after = (t_right[0] + t_right[1]) + (t_right[2] + t_right[3])
    result = mask[...].astype(F32) * (result + from_after * s_after + from_before * s_before)

    mine = rows_of(lev)
    out_buf[mine, :] = result
    gathers = [
        send(out_buf.at[mine], out_buf.at[mine], ag_send.at[k], ag_recv.at[lev], lev ^ k, tile) for k in range(1, 4)
    ]
    for copy in gathers:
        copy.start()

    halo(0).wait_send()
    for k in range(1, 4):
        @pl.when(lev >= k)
        def _():
            halo(k).wait_send()
            down(k).wait_send()
    for copy in edges + t_sends:
        copy.wait_send()
    for i in range(4):
        c = lax.rem(lev + 1 + i, 4)
        if i < 3:
            du(i, c).wait_send()
            self_(i, c).wait_send()
        left(c).wait_send()
        right(c).wait_send()

    for k in range(1, 4):
        d = lev ^ k
        arrived(out_buf.at[rows_of(d)], ag_recv.at[d])
    hess_out[...] = out_buf[...]
    for copy in gathers:
        copy.wait_send()


def per_device(
    control, emit_mask, bin_profile, plume_profile, courant, upwind, bin_speed, level_factor, background, coag_rate,
    obs_weight, obs_precision,
):
    nb, nl, _, ny = background.shape
    total = level_factor.shape[0]
    chunk = nb // 4
    vmem, dma = pltpu.VMEM, pltpu.SemaphoreType.DMA
    obs, hess = pl.pallas_call(
        functools.partial(kernel, nb, nl, total, 1.0 / (nb * total)),
        out_shape=(jax.ShapeDtypeStruct((1, ny), F32), jax.ShapeDtypeStruct((nb, ny), F32)),
        in_specs=[pl.BlockSpec(memory_space=pl.ANY)] * 12,
        out_specs=(pl.BlockSpec(memory_space=pltpu.VMEM),) * 2,
        scratch_shapes=[
            vmem((nl, nb, ny), F32),
            vmem((nb, ny), F32),
            vmem((1, ny), jnp.int32),
            vmem((1, nb), F32),
            vmem((1, nl), F32),
            vmem((2, nl, ny), F32),
            vmem((2, nl, ny), jnp.int32),
            vmem((1, nb), F32),
            vmem((1, total), F32),
            vmem((nl, ny), F32),
            vmem((1, nb), F32),
            vmem((1, ny), F32),
            vmem((2 * nb, 256), BF16),
            vmem((nl, nb, ny), F32),
            vmem((nl + 1, nb, 128), F32),
            vmem((nl, nb, 128), F32),
            vmem((nl, nb, ny), F32),
            vmem((3, total, ny), F32),
            vmem((total, ny), F32),
            vmem((4, total, ny), F32),
            vmem((2, total, ny), F32),
            vmem((4, nb, ny), F32),
            vmem((2, nb, ny), F32),
            vmem((3, nb, ny), F32),
            vmem((2, nb, ny), F32),
            vmem((4, 5, chunk, ny), F32),
            vmem((4, 2, chunk, ny), F32),
            vmem((4, chunk, ny), F32),
            vmem((4, chunk, ny), F32),
            vmem((4, chunk, ny), F32),
            vmem((4, 1, ny), F32),
            vmem((4, 1, ny), F32),
            vmem((4, 1, ny), F32),
            vmem((1, ny), F32),
            vmem((1, ny), F32),
            vmem((nb, ny), F32),
            dma((11,)), dma((nl,)),
            dma((4,)), dma((4,)), dma((4,)), dma((4,)), dma((2,)), dma((2,)),
            dma((4,)), dma((4,)), dma((4,)), dma((4,)), dma((4,)), dma((4,)), dma((4,)), dma((4,)),
            dma((4,)), dma((4,)), dma((8,)), dma((8,)), dma((4,)), dma((4,)),
        ],
        compiler_params=pltpu.CompilerParams(collective_id=0, has_side_effects=True, vmem_limit_bytes=48 << 20),
        name="hessian",
    )(
        control, emit_mask, bin_profile[None], plume_profile[None], courant, upwind, bin_speed[None], level_factor[None],
        background, coag_rate, obs_weight[None], obs_precision,
    )
    return obs, hess[:, None, :]


def solution(mesh):
    in_specs = (
        P(None, "tile", None), P("tile", None), P(), P("lev"), P(None, "lev", "tile", None), P(None, "lev", "tile", None),
        P(), P(), P(None, "lev", "tile", None), P("lev", "tile", None), P(), P("tile", None),
    )
    out_specs = (P("tile", None), P(None, "tile", None))
    return jax.shard_map(per_device, mesh=mesh, in_specs=in_specs, out_specs=out_specs, check_vma=False)
```

profile of v0, /device:TPU:1, one launch (start us, length us, event | category | flops | bytes accessed | tf_op | source)
XLA Modules:
  0.0 43.4 jit_solution(8723154736623220482)
XLA Ops:
  0.6 0.0 copy-start
  0.6 1.4 %copy-done = f32[96,16,1,256]{3,2,1,0:T(1,128)S(1)} copy-done((f32[96,16,1,256]{3,2,1,0:T(1,128)S(1)}, f32[96,16,1,256]{3,2,1,0:T(1,128)}, u32[]{:S(2)}) %copy-start) | copy-done | bytes 1572888
  2.0 0.0 copy-start.1
  2.0 0.9 %copy-done.1 = f32[96,1,256]{2,1,0:T(1,128)S(1)} copy-done((f32[96,1,256]{2,1,0:T(1,128)S(1)}, f32[96,1,256]{2,1,0:T(1,128)}, u32[]{:S(2)}) %copy-start.1) | copy-done | bytes 98328
  2.9 0.0 copy-start.2
  2.9 0.8 %copy-done.2 = f32[2,16,1,256]{3,2,1,0:T(1,128)S(1)} copy-done((f32[2,16,1,256]{3,2,1,0:T(1,128)S(1)}, f32[2,16,1,256]{3,2,1,0:T(1,128)}, u32[]{:S(2)}) %copy-start.2) | copy-done | bytes 32792
  3.7 0.0 copy-start.3
  3.7 0.8 %copy-done.3 = s32[2,16,1,256]{3,2,1,0:T(1,128)S(1)} copy-done((s32[2,16,1,256]{3,2,1,0:T(1,128)S(1)}, s32[2,16,1,256]{3,2,1,0:T(1,128)}, u32[]{:S(2)}) %copy-start.3) | copy-done | bytes 32792
  4.5 0.0 copy-start.4
  4.5 0.7 %copy-done.4 = f32[16,1,256]{2,1,0:T(1,128)S(1)} copy-done((f32[16,1,256]{2,1,0:T(1,128)S(1)}, f32[16,1,256]{2,1,0:T(1,128)}, u32[]{:S(2)}) %copy-start.4) | copy-done | bytes 16408
  5.2 0.0 copy-start.5
  5.2 0.7 %copy-done.5 = s32[1,256]{1,0:T(1,128)S(1)} copy-done((s32[1,256]{1,0:T(1,128)S(1)}, s32[1,256]{1,0:T(1,128)}, u32[]{:S(2)}) %copy-start.5) | copy-done | bytes 1048
  5.9 0.0 copy-start.6
  5.9 0.7 %copy-done.6 = f32[1,256]{1,0:T(1,128)S(1)} copy-done((f32[1,256]{1,0:T(1,128)S(1)}, f32[1,256]{1,0:T(1,128)}, u32[]{:S(2)}) %copy-start.6) | copy-done | bytes 1048
  6.5 0.0 copy-start.7
  6.5 0.7 %copy-done.7 = f32[96]{0:T(128)S(1)} copy-done((f32[96]{0:T(128)S(1)}, f32[96]{0:T(128)}, u32[]{:S(2)}) %copy-start.7) | copy-done | bytes 408
  7.2 0.0 copy-start.8
  7.2 0.7 %copy-done.8 = f32[16]{0:T(128)S(1)} copy-done((f32[16]{0:T(128)S(1)}, f32[16]{0:T(128)}, u32[]{:S(2)}) %copy-start.8) | copy-done | bytes 88
  7.8 0.0 copy-start.9
  7.8 0.7 %copy-done.9 = f32[96]{0:T(128)S(1)} copy-done((f32[96]{0:T(128)S(1)}, f32[96]{0:T(128)}, u32[]{:S(2)}) %copy-start.9) | copy-done | bytes 408
  8.5 0.0 copy-start.10
  8.5 0.7 %copy-done.10 = f32[64]{0:T(128)S(1)} copy-done((f32[64]{0:T(128)S(1)}, f32[64]{0:T(128)}, u32[]{:S(2)}) %copy-start.10) | copy-done | bytes 280
  9.2 0.0 copy-start.11
  9.2 0.7 %copy-done.11 = f32[96]{0:T(128)S(1)} copy-done((f32[96]{0:T(128)S(1)}, f32[96]{0:T(128)}, u32[]{:S(2)}) %copy-start.11) | copy-done | bytes 408
  9.8 32.2 %hessian.1 = (f32[1,256]{1,0:T(1,128)S(1)}, f32[96,256]{1,0:T(8,128)S(1)}) custom-call(f32[96,1,256]{2,1,0:T(1,128)S(1)} %copy-done.1, s32[1,256]{1,0:T(1,128)S(1)} %copy-done.5, f32[1,96]{1,0:T(1,128)S(1)} %bitcast.7, f32[1,16]{1,0:T(1,128)S(1)} %bitcast.8, f32[2,16,1,256]{3,2,1,0:T(1,128)S(1)} %copy-done.2, s32[2,16,1,256]{3,2,1,0:T(1,128)S(1)} %copy-done.3, ...), custom_call_target="tpu_custom_call" | custom-call | tf_op jit(solution)/shard_map/hessian/pallas_call | solution.py:358
  42.0 0.7 %copy.14 = f32[96,1,256]{2,1,0:T(1,128)} copy(f32[96,1,256]{2,0,1:T(8,128)S(1)} %bitcast.6) | data formatting | bytes 196608
  42.8 0.6 %copy.16 = f32[1,256]{1,0:T(1,128)} copy(f32[1,256]{1,0:T(1,128)S(1)} %get-tuple-element.10) | data formatting | bytes 2048
Async XLA Ops:
  0.6 1.4 %copy-start = (f32[96,16,1,256]{3,2,1,0:T(1,128)S(1)}, f32[96,16,1,256]{3,2,1,0:T(1,128)}, u32[]{:S(2)}) copy-start(f32[96,16,1,256]{3,2,1,0:T(1,128)} %background.1) | copy-start | bytes 4718596
  2.0 0.9 %copy-start.1 = (f32[96,1,256]{2,1,0:T(1,128)S(1)}, f32[96,1,256]{2,1,0:T(1,128)}, u32[]{:S(2)}) copy-start(f32[96,1,256]{2,1,0:T(1,128)} %control.1) | copy-start | bytes 294916
  2.9 0.8 %copy-start.2 = (f32[2,16,1,256]{3,2,1,0:T(1,128)S(1)}, f32[2,16,1,256]{3,2,1,0:T(1,128)}, u32[]{:S(2)}) copy-start(f32[2,16,1,256]{3,2,1,0:T(1,128)} %courant.1) | copy-start | bytes 98308
  3.7 0.8 %copy-start.3 = (s32[2,16,1,256]{3,2,1,0:T(1,128)S(1)}, s32[2,16,1,256]{3,2,1,0:T(1,128)}, u32[]{:S(2)}) copy-start(s32[2,16,1,256]{3,2,1,0:T(1,128)} %upwind.1) | copy-start | bytes 98308
  4.5 0.7 %copy-start.4 = (f32[16,1,256]{2,1,0:T(1,128)S(1)}, f32[16,1,256]{2,1,0:T(1,128)}, u32[]{:S(2)}) copy-start(f32[16,1,256]{2,1,0:T(1,128)} %rate_in.1) | copy-start | bytes 49156
  5.2 0.7 %copy-start.5 = (s32[1,256]{1,0:T(1,128)S(1)}, s32[1,256]{1,0:T(1,128)}, u32[]{:S(2)}) copy-start(s32[1,256]{1,0:T(1,128)} %mask_in.1) | copy-start | bytes 3076
  5.9 0.7 %copy-start.6 = (f32[1,256]{1,0:T(1,128)S(1)}, f32[1,256]{1,0:T(1,128)}, u32[]{:S(2)}) copy-start(f32[1,256]{1,0:T(1,128)} %prec_in.1) | copy-start | bytes 3076
  6.5 0.7 %copy-start.7 = (f32[96]{0:T(128)S(1)}, f32[96]{0:T(128)}, u32[]{:S(2)}) copy-start(f32[96]{0:T(128)} %param.14) | copy-start | bytes 1156
  7.2 0.7 %copy-start.8 = (f32[16]{0:T(128)S(1)}, f32[16]{0:T(128)}, u32[]{:S(2)}) copy-start(f32[16]{0:T(128)} %param.15) | copy-start | bytes 196
  7.8 0.7 %copy-start.9 = (f32[96]{0:T(128)S(1)}, f32[96]{0:T(128)}, u32[]{:S(2)}) copy-start(f32[96]{0:T(128)} %param.18) | copy-start | bytes 1156
  8.5 0.7 %copy-start.10 = (f32[64]{0:T(128)S(1)}, f32[64]{0:T(128)}, u32[]{:S(2)}) copy-start(f32[64]{0:T(128)} %param.19) | copy-start | bytes 772
  9.2 0.7 %copy-start.11 = (f32[96]{0:T(128)S(1)}, f32[96]{0:T(128)}, u32[]{:S(2)}) copy-start(f32[96]{0:T(128)} %param.22) | copy-start | bytes 1156
where the time goes:
time: 43.8 us; the launch traced here: 43.4 us
  Pallas kernels  32.2 us (74%)
  local copies, waits for them, and re-layouts  10.5 us (24%)
  between operations  0.66 us (2%)
    pallas_call x1, Pallas kernels, per_device(): pl.pallas_call(functools.partial(kernel, nb, nl, total, 1.0 / (nb * total...  32.2 us
    unnamed x26, local copies, waits for them, and re-layouts  10.5 us

commit v1 on v0

--- a/solution.py
+++ b/solution.py
@@ -67,6 +67,13 @@
     def arrived(dst, sem):
         pltpu.make_async_copy(dst, dst, sem).wait()
 
+    barrier = pltpu.get_barrier_semaphore()
+    for near in (before, after):
+        for k in range(4):
+            pl.semaphore_signal(barrier, inc=1, device_id=at(k, near), device_id_type=MESH)
+    for k in range(1, 4):
+        pl.semaphore_signal(barrier, inc=1, device_id=at(lev ^ k, tile), device_id_type=MESH)
+
     small = [
         (courant.at[:, :, 0, :], cour), (upwind.at[:, :, 0, :], upw), (plume_in, plume), (control.at[:, 0, :], ctl),
         (mask_in, mask), (speed_in, speed), (factor_in, factor), (weight_in, weight), (profile_in, profile),
@@ -84,13 +91,6 @@
         return 0
 
     lax.fori_loop(0, nl, bg_start, 0)
-
-    barrier = pltpu.get_barrier_semaphore()
-    for k in range(1, 4):
-        pl.semaphore_signal(barrier, inc=1, device_id=at(lev ^ k, tile), device_id_type=MESH)
-    for near in (before, after):
-        for k in range(4):
-            pl.semaphore_signal(barrier, inc=1, device_id=at(k, near), device_id_type=MESH)
 
     for n in range(3):
         loads[n].wait()
@@ -402,12 +402,14 @@
             dma((4,)), dma((4,)), dma((4,)), dma((4,)), dma((4,)), dma((4,)), dma((4,)), dma((4,)),
             dma((4,)), dma((4,)), dma((8,)), dma((8,)), dma((4,)), dma((4,)),
         ],
-        compiler_params=pltpu.CompilerParams(collective_id=0, has_side_effects=True, vmem_limit_bytes=48 << 20),
+        compiler_params=pltpu.CompilerParams(collective_id=0, has_side_effects=True, vmem_limit_bytes=24 << 20),
         name="hessian",
-    )(
-        control, emit_mask, bin_profile[None], plume_profile[None], courant, upwind, bin_speed[None], level_factor[None],
-        background, coag_rate, obs_weight[None], obs_precision,
-    )
+    )(*[
+        pltpu.with_memory_space_constraint(value, pltpu.HBM) for value in (
+            control, emit_mask, bin_profile[None], plume_profile[None], courant, upwind, bin_speed[None],
+            level_factor[None], background, coag_rate, obs_weight[None], obs_precision,
+        )
+    ])
     return obs, hess[:, None, :]
 
 

time: 43.8 us -> 33 us (0.75)
  local copies, waits for them, and re-layouts: 10.5 us -> 1.3 us
  Pallas kernels: 32.2 us -> 30.9 us
    unnamed x26 -> x2, local copies, waits for them, and re-layouts: 10.5 us -> 1.3 us
    pallas_call x1, Pallas kernels: 32.2 us -> 30.9 us  [per_device(): pl.pallas_call(functools.partial(kernel, nb, nl, total, 1.0 / (nb * total...]
where the time goes in v1:
time: 33 us; the launch traced here: 32.9 us
  Pallas kernels  30.9 us (94%)
  local copies, waits for them, and re-layouts  1.3 us (4%)
  between operations  0.64 us (2%)
    pallas_call x1, Pallas kernels, per_device(): pl.pallas_call(functools.partial(kernel, nb, nl, total, 1.0 / (nb * total...  30.9 us
    unnamed x2, local copies, waits for them, and re-layouts  1.3 us

profile of v1, /device:TPU:1, one launch (start us, length us, event | category | flops | bytes accessed | tf_op | source)
XLA Modules:
  0.0 32.9 jit_solution(11669555868341416692)
XLA Ops:
  0.6 30.9 %hessian.1 = (f32[1,256]{1,0:T(1,128)S(1)}, f32[96,256]{1,0:T(8,128)S(1)}) custom-call(f32[96,1,256]{2,1,0:T(1,128)} %control.1, s32[1,256]{1,0:T(1,128)} %mask_in.1, f32[1,96]{1,0:T(1,128)} %bitcast.7, f32[1,16]{1,0:T(1,128)} %bitcast.8, f32[2,16,1,256]{3,2,1,0:T(1,128)} %courant.1, s32[2,16,1,256]{3,2,1,0:T(1,128)} %upwind.1, f32[1,96]{1,0:T(1,128)} %bitcast.9, ...), custom_call_target="tpu_custom_call" | custom-call | tf_op jit(solution)/shard_map/hessian/pallas_call | solution.py:358
  31.5 0.7 %copy.14 = f32[96,1,256]{2,1,0:T(1,128)} copy(f32[96,1,256]{2,0,1:T(8,128)S(1)} %bitcast.6) | data formatting | bytes 196608
  32.3 0.6 %copy.16 = f32[1,256]{1,0:T(1,128)} copy(f32[1,256]{1,0:T(1,128)S(1)} %get-tuple-element.10) | data formatting | bytes 2048

commit v2 on v1

--- a/solution.py
+++ b/solution.py
@@ -116,17 +116,19 @@
     def down(k):
         return send(face.at[:, pl.ds(0, nl)], face.at[:, pl.ds(k * nl, nl)], down_send.at[k], down_recv.at[k], lev - k, tile)
 
+    lev_after = lev ^ jnp.where(lax.rem(tile, 8) == 7, 2, 0)
+    lev_before = lev ^ jnp.where(lax.rem(tile, 8) == 0, 2, 0)
     edges = [
-        send(masked.at[0], edge.at[0], edge_send.at[0], edge_recv.at[0], lev, after),
-        send(masked.at[0], edge.at[1], edge_send.at[1], edge_recv.at[1], lev, before),
+        send(masked.at[0], edge.at[0], edge_send.at[0], edge_recv.at[0], lev_after, after),
+        send(masked.at[0], edge.at[1], edge_send.at[1], edge_recv.at[1], lev_before, before),
     ]
     halo(0).start()
     for k in range(1, 4):
         @pl.when(lev >= k)
         def _():
             halo(k).start()
-    for copy in edges:
-        copy.start()
+    edges[1].start()
+    edges[0].start()
     for k in range(1, 4):
         @pl.when(lev >= k)
         def _():
@@ -241,8 +243,6 @@
     ncoef[1] = -jnp.minimum(nface[...], 0.0)
     for n in range(2):
         nquot[n] = dot3(chain, ncoef[n])
-    for n in range(2):
-        arrived(edge.at[n], edge_recv.at[n])
 
     def finish(i, t_sum):
         c = lax.rem(lev + 1 + i, 4)
@@ -263,15 +263,19 @@
         def _():
             self_(i, c).start()
         right(c).start()
-        part = (
-            masked[0, rows, :] * k_self + edge[0, rows, :] * kern[c, 2] + edge[1, rows, :] * k_right
-            + masked[1, rows, :] * kern[c, 0] + masked[2, rows, :] * kern[c, 1]
-        )
+        part = masked[0, rows, :] * k_self + masked[1, rows, :] * kern[c, 0] + masked[2, rows, :] * kern[c, 1]
         for r in range(0, chunk, 8):
             t_sum = t_sum + part[r:r + 8]
         return t_sum
 
     t_sum = lax.fori_loop(0, 4, finish, jnp.zeros((8, ny), F32))
+    for n in range(2):
+        arrived(edge.at[n], edge_recv.at[n])
+    for c in range(4):
+        rows = pl.ds(c * chunk, chunk)
+        part = edge[0, rows, :] * kern[c, 2] + edge[1, rows, :] * kern[c, 4]
+        for r in range(0, chunk, 8):
+            t_sum = t_sum + part[r:r + 8]
     t_mine = jnp.sum(t_sum, axis=0, keepdims=True) * scale
     s_mine = t_mine * prec[...] * scale
     t_own[...] = t_mine

time: 33 us -> 30.6 us (0.927)
  Pallas kernels: 30.9 us -> 28.6 us
    pallas_call x1, Pallas kernels: 30.9 us -> 28.6 us  [per_device(): pl.pallas_call(functools.partial(kernel, nb, nl, total, 1.0 / (nb * total...]
where the time goes in v2:
time: 30.6 us; the launch traced here: 30.5 us
  Pallas kernels  28.6 us (93%)
  local copies, waits for them, and re-layouts  1.3 us (4%)
  between operations  0.64 us (2%)
    pallas_call x1, Pallas kernels, per_device(): pl.pallas_call(functools.partial(kernel, nb, nl, total, 1.0 / (nb * total...  28.6 us
    unnamed x2, local copies, waits for them, and re-layouts  1.3 us

profile of v2, /device:TPU:1, one launch (start us, length us, event | category | flops | bytes accessed | tf_op | source)
XLA Modules:
  0.0 30.5 jit_solution(907210583461196693)
XLA Ops:
  0.6 28.6 %hessian.1 = (f32[1,256]{1,0:T(1,128)S(1)}, f32[96,256]{1,0:T(8,128)S(1)}) custom-call(f32[96,1,256]{2,1,0:T(1,128)} %control.1, s32[1,256]{1,0:T(1,128)} %mask_in.1, f32[1,96]{1,0:T(1,128)} %bitcast.7, f32[1,16]{1,0:T(1,128)} %bitcast.8, f32[2,16,1,256]{3,2,1,0:T(1,128)} %courant.1, s32[2,16,1,256]{3,2,1,0:T(1,128)} %upwind.1, f32[1,96]{1,0:T(1,128)} %bitcast.9, ...), custom_call_target="tpu_custom_call" | custom-call | tf_op jit(solution)/shard_map/hessian/pallas_call | solution.py:362
  29.2 0.7 %copy.14 = f32[96,1,256]{2,1,0:T(1,128)} copy(f32[96,1,256]{2,0,1:T(8,128)S(1)} %bitcast.6) | data formatting | bytes 196608
  30.0 0.6 %copy.16 = f32[1,256]{1,0:T(1,128)} copy(f32[1,256]{1,0:T(1,128)S(1)} %get-tuple-element.10) | data formatting | bytes 2048

commit v3 on v2

v3 whole, which is shorter than its diff:
```python
import functools

import jax
import jax.numpy as jnp
from jax import lax
from jax.experimental import pallas as pl
from jax.experimental.pallas import tpu as pltpu
from jax.sharding import PartitionSpec as P

MESH = pl.DeviceIdType.MESH
F32, BF16 = jnp.float32, jnp.bfloat16


def split(value):
    high = value.astype(BF16)
    return high, (value - high.astype(F32)).astype(BF16)


def dot3(a, b):
    a_hi, a_lo = split(a)
    b_hi, b_lo = split(b)
    dot = functools.partial(jnp.dot, preferred_element_type=F32)
    return dot(a_hi, b_hi) + (dot(a_hi, b_lo) + dot(a_lo, b_hi))


def iota(shape, dim):
    return lax.broadcasted_iota(jnp.int32, shape, dim)


def pad_row(row, lanes):
    return jnp.concatenate([row, jnp.zeros((1, lanes - row.shape[1]), row.dtype)], axis=1)


def column(row, rows):
    shape = (rows, row.shape[1])
    picked = jnp.where(iota(shape, 0) == iota(shape, 1), jnp.broadcast_to(row, shape), 0.0)
    return jnp.sum(picked, axis=1, keepdims=True)


def kernel(
    nb, nl, total, scale,
    control, mask_in, profile_in, plume_in, courant, upwind, speed_in, factor_in, background, rate_in, weight_in, prec_in,
    obs_out, hess_out,
    bg, ctl, mask, profile, plume, cour, upw, speed, factor, rate, weight, prec,
    lhs, amp, rb, gb, bfield, face, nface, coef, ncoef, here, nhere, quot, nquot, masked, edge, kern,
    krow, mine_in, left_in, right_in, part_in, t_lev, t_left, t_right, t_own, s_own, out_buf,
    load_sem, bg_sem,
    halo_send, halo_recv, down_send, down_recv, edge_send, edge_recv,
    mine_send, mine_recv, left_send, left_recv, right_send, right_recv,
    part_send, part_recv, tl_send, tl_recv, tx_send, tx_recv, ag_send, ag_recv, near_sem, far_sem, entry_sem,
):
    lev, tile = lax.axis_index("lev"), lax.axis_index("tile")
    tiles = lax.axis_size("tile")
    before, after = lax.rem(tile + tiles - 1, tiles), lax.rem(tile + 1, tiles)
    ny = bg.shape[2]
    chunk = nb // 4
    run = min(8, tiles)
    place = lax.rem(tile, run)
    is_first, is_last = place == 0, place == run - 1
    lev_after = lev ^ jnp.where(is_last, 2, 0)
    lev_before = lev ^ jnp.where(is_first, 2, 0)
    core = lax.rem(lev, 2)
    own = pl.ds(pl.multiple_of(lev * nl, 8), nl)

    def at(lev_to, tile_to):
        return {"lev": lev_to, "tile": tile_to}

    def send(src, dst, send_sem, recv_sem, lev_to, tile_to):
        return pltpu.make_async_remote_copy(
            src_ref=src, dst_ref=dst, send_sem=send_sem, recv_sem=recv_sem,
            device_id=at(lev_to, tile_to), device_id_type=MESH,
        )

    def arrived(dst, sem):
        pltpu.make_async_copy(dst, dst, sem).wait()

    barrier = pltpu.get_barrier_semaphore()

    @pl.when(is_last)
    def _():
        pl.semaphore_wait(barrier, 4)
        for n in range(2):
            pl.semaphore_signal(near_sem, inc=1, device_id=at(lev_after - core + n, after), device_id_type=MESH)
        for n in range(2):
            pl.semaphore_signal(far_sem, inc=1, device_id=at(lev - core + n, after), device_id_type=MESH)

    for k in range(4):
        pl.semaphore_signal(barrier, inc=1, device_id=at(k, before), device_id_type=MESH)

    @pl.when(place < run - 2)
    def _():
        for k in range(4):
            pl.semaphore_signal(barrier, inc=1, device_id=at(k, after), device_id_type=MESH)

    @pl.when(jnp.logical_not(is_last))
    def _():
        for k in range(1, 4):
            pl.semaphore_signal(barrier, inc=1, device_id=at(lev ^ k, tile), device_id_type=MESH)

    small = [
        (courant.at[:, :, 0, :], cour), (upwind.at[:, :, 0, :], upw), (plume_in, plume), (control.at[:, 0, :], ctl),
        (mask_in, mask), (speed_in, speed), (factor_in, factor), (weight_in, weight), (profile_in, profile),
        (rate_in.at[:, 0, :], rate), (prec_in, prec),
    ]
    loads = [pltpu.make_async_copy(a, b, load_sem.at[n]) for n, (a, b) in enumerate(small)]
    for copy in loads:
        copy.start()

    def bg_copy(l):
        return pltpu.make_async_copy(background.at[:, l, 0, :], bg.at[l], bg_sem.at[l])

    def bg_start(l, _):
        bg_copy(l).start()
        return 0

    lax.fori_loop(0, nl, bg_start, 0)

    @pl.when(is_first)
    def _():
        pl.semaphore_wait(barrier, 7)

    @pl.when(jnp.logical_not(jnp.logical_or(is_first, is_last)))
    def _():
        pl.semaphore_wait(barrier, 11)

    @pl.when(place == run - 2)
    def _():
        for k in range(4):
            pl.semaphore_signal(entry_sem, inc=1, device_id=at(k, after), device_id_type=MESH)

    for n in range(3):
        loads[n].wait()
    plume_col = column(plume[...], nl)
    scaled = jnp.where(upw[...] == 1, cour[...], -cour[...]) * plume_col[None]
    face[0, own, :] = scaled[0]
    face[1, own, :] = scaled[1]
    face[2, own, :] = jnp.broadcast_to(plume_col, (nl, ny))
    for m in range(3):
        @pl.when(m < lev)
        def _():
            nface[m * nl:(m + 1) * nl, :] = jnp.zeros((nl, ny), F32)
    for n in range(3, 5):
        loads[n].wait()
    masked[0] = ctl[...] * mask[...].astype(F32)

    def upward(d):
        return pl.ds(d * nl, total - d * nl)

    def halo(d):
        return send(face.at[0, upward(d)], nface.at[upward(d)], halo_send.at[0], halo_recv.at[0], lev_before, before)

    def spread(k):
        return send(face.at[:, own], face.at[:, own], down_send.at[k], down_recv.at[lev], lev ^ k, tile)

    edges = [
        send(masked.at[0], edge.at[0], edge_send.at[0], edge_recv.at[0], lev_after, after),
        send(masked.at[0], edge.at[1], edge_send.at[1], edge_recv.at[1], lev_before, before),
    ]

    @pl.when(is_last)
    def _():
        edges[0].start()
        pl.semaphore_wait(entry_sem, 4)

    for k in range(1, 4):
        spread(k).start()

    @pl.when(jnp.logical_not(is_last))
    def _():
        edges[0].start()

    @pl.when(jnp.logical_not(is_first))
    def _():
        edges[1].start()

    for n in range(5, 11):
        loads[n].wait()
    row_i, lane_i = iota((nb, 128), 0), iota((nb, 128), 1)
    weight_row = pad_row(weight[...], 128)
    weight_col = column(weight_row, nb)
    shifted = jnp.broadcast_to(weight_row, (nb, 128))
    for bit in range(7):
        shifted = jnp.where((row_i >> bit) & 1 == 1, pltpu.roll(shifted, 128 - (1 << bit), 1), shifted)
    mixing = jnp.where(row_i + lane_i < nb, shifted, 0.0) - weight_row - weight_col
    mix_hi, mix_lo = split(jnp.where(lane_i < nb, mixing, 0.0))
    lhs[0:nb, 0:128] = mix_hi
    lhs[0:nb, 128:256] = mix_hi
    lhs[nb:2 * nb, 0:128] = mix_lo
    lhs[nb:2 * nb, 128:256] = jnp.zeros((nb, 128), BF16)

    speed_col = column(pad_row(speed[...], 128), nb)
    profile_col = column(pad_row(profile[...], 128), nb)
    factor_row = pad_row(factor[...], 128)
    fall = speed_col * factor_row
    above = fall / (1.0 + fall)
    fall = speed_col * pltpu.roll(jnp.broadcast_to(factor_row, (8, 128)), lax.rem(128 - lev * nl, 128), 1)[0:1]
    inverse = 1.0 / (1.0 + fall)
    gain = fall * inverse
    for l in range(nl):
        rb[l] = jnp.broadcast_to(inverse[:, l:l + 1], (nb, 128))
        gb[l] = jnp.broadcast_to(gain[:, l:l + 1], (nb, 128))
    chain = jnp.where(lane_i < (lev + 1) * nl, 1.0, above)
    step = 1
    while step < total:
        chain = chain * jnp.where(lane_i >= step, pltpu.roll(chain, step, 1), 1.0)
        step *= 2
    chain = jnp.where(lane_i < (lev + 1) * nl, 0.0, chain)[:, 0:total]

    masked[1] = pltpu.roll(masked[0], 1, 1)
    masked[2] = pltpu.roll(masked[0], ny - 1, 1)

    def mix_level(l, _):
        bg_copy(l).wait()
        hi, lo = split(bg[l])
        rest = jnp.zeros((128 - nb, ny), BF16)
        both = jnp.dot(lhs[...], jnp.concatenate([hi, rest, lo, rest], axis=0), preferred_element_type=F32)
        amp[l] = weight_col + rate[pl.ds(l, 1), :] * (both[0:nb] + both[nb:2 * nb])
        return 0

    lax.fori_loop(0, nl, mix_level, 0)

    def rows_of(c):
        return pl.ds(pl.multiple_of(c * chunk, 8), chunk)

    def wide(value):
        return jnp.concatenate([value] * (ny // 128), axis=1)

    rb[nl] = jnp.broadcast_to(profile_col, (nb, 128))

    def settle(c, _):
        rows = rows_of(c)
        value = jnp.zeros((chunk, ny), F32)
        for l in range(nl):
            value = amp[l, rows, :] * wide(rb[l, rows, :]) + value * wide(gb[l, rows, :])
            bfield[l, rows, :] = value
        return 0

    lax.fori_loop(0, 4, settle, 0)

    def faces():
        for k in range(1, 4):
            d = lev ^ k
            arrived(face.at[:, pl.ds(pl.multiple_of(d * nl, 8), nl)], down_recv.at[d])

    def send_halos():
        for d in range(4):
            @pl.when(d == lev_before)
            def _():
                halo(d).start()

    @pl.when(jnp.logical_not(is_last))
    def _():
        faces()

    @pl.when(is_first)
    def _():
        pl.semaphore_wait(near_sem, 2)

    @pl.when(jnp.logical_not(is_last))
    def _():
        send_halos()

    @pl.when(is_first)
    def _():
        edges[1].start()
        pl.semaphore_wait(far_sem, 2)

    for d in range(4):
        @pl.when(d == lev)
        def _():
            arrived(nface.at[upward(d)], halo_recv.at[0])
    inflow = -jnp.minimum(nface[...], 0.0)
    ncoef[...] = inflow
    nhere[...] = ncoef[own, :]
    nquot[...] = dot3(chain, inflow)

    def right(c):
        part = lax.rem(c, 2)
        return send(
            krow.at[rows_of(c)], right_in.at[part, core], right_send.at[c], right_recv.at[2 * part + core],
            lev_after - core + c // 2, after,
        )

    def next_row(i, _):
        c = lax.rem(2 * i, 4) + i // 2
        rows = rows_of(c)
        total_in = jnp.zeros((chunk, ny), F32)
        for l in range(nl):
            total_in = total_in + bfield[l, rows, :] * nhere[l:l + 1, :]
        krow[rows, :] = wide(rb[nl, rows, :]) * (total_in + bfield[nl - 1, rows, :] * nquot[rows, :])
        right(c).start()
        return 0

    lax.fori_loop(0, 4, next_row, 0)

    @pl.when(is_last)
    def _():
        faces()
        send_halos()

    face_x, face_y = face[0], face[1]
    next_y = pltpu.roll(face_y, ny - 1, 1)
    coef[0] = jnp.maximum(face_y, 0.0)
    coef[1] = -jnp.minimum(next_y, 0.0)
    coef[2] = (
        face[2] + jnp.minimum(face_x, 0.0) + jnp.minimum(face_y, 0.0) - jnp.maximum(next_y, 0.0)
        - jnp.maximum(nface[...], 0.0)
    )
    coef[3] = jnp.maximum(face_x, 0.0)
    for n in range(4):
        quot[n] = dot3(chain, coef[n])
        here[n] = coef[n, own, :]

    def mine_to(c):
        return send(kern.at[c, pl.ds(0, 3)], mine_in.at[lev], mine_send.at[c], mine_recv.at[lev], c, tile)

    def left(c):
        return send(kern.at[c, 3], left_in.at[lev], left_send.at[c], left_recv.at[lev], c, before)

    def others(c, t_sum):
        rows = rows_of(c)
        sums = [jnp.zeros((chunk, ny), F32) for _ in range(4)]
        for l in range(nl):
            value = bfield[l, rows, :]
            for n in range(4):
                sums[n] = sums[n] + value * here[n, l:l + 1, :]
        prof = wide(rb[nl, rows, :])
        value = bfield[nl - 1, rows, :]
        sums = [prof * (sums[n] + value * quot[n, rows, :]) for n in range(4)]
        for n in range(4):
            kern[c, n] = sums[n]

        @pl.when(c != lev)
        def _():
            mine_to(c).start()
        left(c).start()
        part = masked[0, rows, :] * sums[2] + masked[1, rows, :] * sums[0] + masked[2, rows, :] * sums[1]
        for r in range(0, chunk, 8):
            t_sum = t_sum + part[r:r + 8]
        return t_sum

    t_sum = lax.fori_loop(0, 4, others, jnp.zeros((8, ny), F32))
    for n in range(2):
        arrived(edge.at[n], edge_recv.at[n])
    for c in range(4):
        rows = pl.ds(c * chunk, chunk)
        part = edge[0, rows, :] * kern[c, 3] + edge[1, rows, :] * krow[rows, :]
        for r in range(0, chunk, 8):
            t_sum = t_sum + part[r:r + 8]
    t_mine = jnp.sum(t_sum, axis=0, keepdims=True) * scale
    s_mine = t_mine * prec[...] * scale
    t_own[...] = t_mine
    s_own[...] = s_mine

    t_sends = []
    for k in range(4):
        t_sends.append(send(s_own, t_left.at[lev], tx_send.at[k], tx_recv.at[lev], k, after))
        t_sends.append(send(s_own, t_right.at[lev], tx_send.at[4 + k], tx_recv.at[4 + lev], k, before))
    for k in range(1, 4):
        t_sends.append(send(t_own, t_lev.at[k], tl_send.at[k], tl_recv.at[k], lev ^ k, tile))
    for copy in t_sends:
        copy.start()

    def part(n, k):
        return send(
            part_in.at[lev, n], part_in.at[lev, n], part_send.at[4 * n + k], part_recv.at[4 * n + lev], lev ^ k, tile
        )

    def from_before():
        for n in range(2):
            for k in range(2):
                arrived(right_in.at[n, k], right_recv.at[2 * n + k])
            part_in[lev, n] = right_in[n, 0] + right_in[n, 1]
            for k in range(1, 4):
                part(n, k).start()

    @pl.when(jnp.logical_not(is_first))
    def _():
        from_before()

    totals = [kern[lev, n] for n in range(3)]
    for k in range(1, 4):
        d = lev ^ k
        arrived(mine_in.at[d], mine_recv.at[d])
        totals = [totals[n] + mine_in[d, n] for n in range(3)]
    t_all = t_mine
    for k in range(1, 4):
        arrived(t_lev.at[k], tl_recv.at[k])
        t_all = t_all + t_lev[k]
    obs_out[...] = t_all
    s_here = t_all * prec[...] * scale
    result = totals[2] * s_here + pltpu.roll(totals[0] * s_here, ny - 1, 1) + pltpu.roll(totals[1] * s_here, 1, 1)
    for k in range(4):
        arrived(left_in.at[k], left_recv.at[k])
    from_after = (left_in[0] + left_in[1]) + (left_in[2] + left_in[3])
    for k in range(4):
        arrived(t_right.at[k], tx_recv.at[4 + k])
    s_after = (t_right[0] + t_right[1]) + (t_right[2] + t_right[3])
    mine = rows_of(lev)
    out_buf[mine, :] = result + from_after * s_after
    gathers = [
        send(out_buf.at[mine], out_buf.at[mine], ag_send.at[k], ag_recv.at[lev], lev ^ k, tile) for k in range(1, 4)
    ]
    for copy in gathers:
        copy.start()

    @pl.when(is_first)
    def _():
        from_before()

    for d in range(4):
        @pl.when(d == lev_before)
        def _():
            halo(d).wait_send()
    for k in range(1, 4):
        spread(k).wait_send()
    for copy in edges + t_sends:
        copy.wait_send()
    for c in range(4):
        @pl.when(c != lev)
        def _():
            mine_to(c).wait_send()
        left(c).wait_send()
        right(c).wait_send()

    for copy in gathers:
        copy.wait_send()

    for k in range(4):
        arrived(t_left.at[k], tx_recv.at[k])
    s_before = (t_left[0] + t_left[1]) + (t_left[2] + t_left[3])
    for k in range(1, 4):
        d = lev ^ k
        arrived(out_buf.at[rows_of(d)], ag_recv.at[d])
    mask_row = mask[...].astype(F32)
    for n in range(2):
        for k in range(1, 4):
            d = lev ^ k
            arrived(part_in.at[d, n], part_recv.at[4 * n + d])
        for h in range(2):
            rows = pl.ds((2 * h + n) * chunk, chunk)
            hess_out[rows, :] = mask_row * (out_buf[rows, :] + (part_in[h, n] + part_in[2 + h, n]) * s_before)
    for n in range(2):
        for k in range(1, 4):
            part(n, k).wait_send()


def per_device(
    control, emit_mask, bin_profile, plume_profile, courant, upwind, bin_speed, level_factor, background, coag_rate,
    obs_weight, obs_precision,
):
    nb, nl, _, ny = background.shape
    total = level_factor.shape[0]
    chunk = nb // 4
    vmem, dma = pltpu.VMEM, pltpu.SemaphoreType.DMA
    obs, hess = pl.pallas_call(
        functools.partial(kernel, nb, nl, total, 1.0 / (nb * total)),
        out_shape=(jax.ShapeDtypeStruct((1, ny), F32), jax.ShapeDtypeStruct((nb, ny), F32)),
        in_specs=[pl.BlockSpec(memory_space=pl.ANY)] * 12,
        out_specs=(pl.BlockSpec(memory_space=pltpu.VMEM),) * 2,
        scratch_shapes=[
            vmem((nl, nb, ny), F32),
            vmem((nb, ny), F32),
            vmem((1, ny), jnp.int32),
            vmem((1, nb), F32),
            vmem((1, nl), F32),
            vmem((2, nl, ny), F32),
            vmem((2, nl, ny), jnp.int32),
            vmem((1, nb), F32),
            vmem((1, total), F32),
            vmem((nl, ny), F32),
            vmem((1, nb), F32),
            vmem((1, ny), F32),
            vmem((2 * nb, 256), BF16),
            vmem((nl, nb, ny), F32),
            vmem((nl + 1, nb, 128), F32),
            vmem((nl, nb, 128), F32),
            vmem((nl, nb, ny), F32),
            vmem((3, total, ny), F32),
            vmem((total, ny), F32),
            vmem((4, total, ny), F32),
            vmem((total, ny), F32),
            vmem((4, nl, ny), F32),
            vmem((nl, ny), F32),
            vmem((4, nb, ny), F32),
            vmem((nb, ny), F32),
            vmem((3, nb, ny), F32),
            vmem((2, nb, ny), F32),
            vmem((4, 4, chunk, ny), F32),
            vmem((nb, ny), F32),
            vmem((4, 3, chunk, ny), F32),
            vmem((4, chunk, ny), F32),
            vmem((2, 2, chunk, ny), F32),
            vmem((4, 2, chunk, ny), F32),
            vmem((4, 1, ny), F32),
            vmem((4, 1, ny), F32),
            vmem((4, 1, ny), F32),
            vmem((1, ny), F32),
            vmem((1, ny), F32),
            vmem((nb, ny), F32),
            dma((11,)), dma((nl,)),
            dma((4,)), dma((4,)), dma((4,)), dma((4,)), dma((2,)), dma((2,)),
            dma((4,)), dma((4,)), dma((4,)), dma((4,)), dma((4,)), dma((4,)),
            dma((8,)), dma((8,)), dma((4,)), dma((4,)), dma((8,)), dma((8,)), dma((4,)), dma((4,)),
            pltpu.SemaphoreType.REGULAR, pltpu.SemaphoreType.REGULAR, pltpu.SemaphoreType.REGULAR,
        ],
        compiler_params=pltpu.CompilerParams(collective_id=0, has_side_effects=True, vmem_limit_bytes=24 << 20),
        name="hessian",
    )(*[
        pltpu.with_memory_space_constraint(value, pltpu.HBM) for value in (
            control, emit_mask, bin_profile[None], plume_profile[None], courant, upwind, bin_speed[None],
            level_factor[None], background, coag_rate, obs_weight[None], obs_precision,
        )
    ])
    return obs, hess[:, None, :]


def solution(mesh):
    in_specs = (
        P(None, "tile", None), P("tile", None), P(), P("lev"), P(None, "lev", "tile", None), P(None, "lev", "tile", None),
        P(), P(), P(None, "lev", "tile", None), P("lev", "tile", None), P(), P("tile", None),
    )
    out_specs = (P("tile", None), P(None, "tile", None))
    return jax.shard_map(per_device, mesh=mesh, in_specs=in_specs, out_specs=out_specs, check_vma=False)
```

time: 30.6 us -> 29.1 us (0.951)
  Pallas kernels: 28.6 us -> 27.1 us
    pallas_call x1, Pallas kernels: 28.6 us -> 27.1 us  [per_device(): pl.pallas_call(functools.partial(kernel, nb, nl, total, 1.0 / (nb * total...]
where the time goes in v3:
time: 29.1 us; the launch traced here: 29 us
  Pallas kernels  27.1 us (93%)
  local copies, waits for them, and re-layouts  1.3 us (4%)
  between operations  0.64 us (2%)
    pallas_call x1, Pallas kernels, per_device(): pl.pallas_call(functools.partial(kernel, nb, nl, total, 1.0 / (nb * total...  27.1 us
    unnamed x2, local copies, waits for them, and re-layouts  1.3 us

profile of v3, /device:TPU:1, one launch (start us, length us, event | category | flops | bytes accessed | tf_op | source)
XLA Modules:
  0.0 29.0 jit_solution(10964153867566121248)
XLA Ops:
  0.6 27.1 %hessian.1 = (f32[1,256]{1,0:T(1,128)S(1)}, f32[96,256]{1,0:T(8,128)S(1)}) custom-call(f32[96,1,256]{2,1,0:T(1,128)} %control.1, s32[1,256]{1,0:T(1,128)} %mask_in.1, f32[1,96]{1,0:T(1,128)} %bitcast.7, f32[1,16]{1,0:T(1,128)} %bitcast.8, f32[2,16,1,256]{3,2,1,0:T(1,128)} %courant.1, s32[2,16,1,256]{3,2,1,0:T(1,128)} %upwind.1, f32[1,96]{1,0:T(1,128)} %bitcast.9, ...), custom_call_target="tpu_custom_call" | custom-call | tf_op jit(solution)/shard_map/hessian/pallas_call | solution.py:456
  27.7 0.7 %copy.14 = f32[96,1,256]{2,1,0:T(1,128)} copy(f32[96,1,256]{2,0,1:T(8,128)S(1)} %bitcast.6) | data formatting | bytes 196608
  28.5 0.6 %copy.16 = f32[1,256]{1,0:T(1,128)} copy(f32[1,256]{1,0:T(1,128)S(1)} %get-tuple-element.10) | data formatting | bytes 2048

commit v4 on v3

--- a/solution.py
+++ b/solution.py
@@ -275,10 +275,14 @@
     nquot[...] = dot3(chain, inflow)
 
     def right(c):
-        part = lax.rem(c, 2)
         return send(
-            krow.at[rows_of(c)], right_in.at[part, core], right_send.at[c], right_recv.at[2 * part + core],
-            lev_after - core + c // 2, after,
+            krow.at[rows_of(c)], right_in.at[0, core], right_send.at[c], right_recv.at[core], lev_after - core + c // 2, after
+        )
+
+    def right_both(c, to):
+        return send(
+            krow.at[rows_of(c)], right_in.at[1, lev], right_send.at[4 + 2 * (c // 2) + to // 2], right_recv.at[4 + lev],
+            to + c // 2, after,
         )
 
     def next_row(i, _):
@@ -288,7 +292,14 @@
         for l in range(nl):
             total_in = total_in + bfield[l, rows, :] * nhere[l:l + 1, :]
         krow[rows, :] = wide(rb[nl, rows, :]) * (total_in + bfield[nl - 1, rows, :] * nquot[rows, :])
-        right(c).start()
+        @pl.when(i < 2)
+        def _():
+            right(c).start()
+
+        @pl.when(i >= 2)
+        def _():
+            for to in (0, 2):
+                right_both(c, to).start()
         return 0
 
     lax.fori_loop(0, 4, next_row, 0)
@@ -367,12 +378,15 @@
         )
 
     def from_before():
-        for n in range(2):
-            for k in range(2):
-                arrived(right_in.at[n, k], right_recv.at[2 * n + k])
-            part_in[lev, n] = right_in[n, 0] + right_in[n, 1]
-            for k in range(1, 4):
-                part(n, k).start()
+        for k in range(2):
+            arrived(right_in.at[0, k], right_recv.at[k])
+        part_in[lev, 0] = right_in[0, 0] + right_in[0, 1]
+        for k in range(1, 4):
+            part(0, k).start()
+        for k in range(4):
+            arrived(right_in.at[1, k], right_recv.at[4 + k])
+        part_in[lev, 1] = (right_in[1, 0] + right_in[1, 1]) + (right_in[1, 2] + right_in[1, 3])
+        part(1, 1).start()
 
     @pl.when(jnp.logical_not(is_first))
     def _():
@@ -414,6 +428,10 @@
             halo(d).wait_send()
     for k in range(1, 4):
         spread(k).wait_send()
+    for h in range(2):
+        right(2 * h).wait_send()
+        for to in (0, 2):
+            right_both(2 * h + 1, to).wait_send()
     for copy in edges + t_sends:
         copy.wait_send()
     for c in range(4):
@@ -421,7 +439,6 @@
         def _():
             mine_to(c).wait_send()
         left(c).wait_send()
-        right(c).wait_send()
 
     for copy in gathers:
         copy.wait_send()
@@ -433,16 +450,19 @@
         d = lev ^ k
         arrived(out_buf.at[rows_of(d)], ag_recv.at[d])
     mask_row = mask[...].astype(F32)
-    for n in range(2):
-        for k in range(1, 4):
-            d = lev ^ k
-            arrived(part_in.at[d, n], part_recv.at[4 * n + d])
-        for h in range(2):
-            rows = pl.ds((2 * h + n) * chunk, chunk)
-            hess_out[rows, :] = mask_row * (out_buf[rows, :] + (part_in[h, n] + part_in[2 + h, n]) * s_before)
-    for n in range(2):
-        for k in range(1, 4):
-            part(n, k).wait_send()
+    arrived(part_in.at[lev ^ 1, 1], part_recv.at[4 + (lev ^ 1)])
+    for h in range(2):
+        rows = pl.ds((2 * h + 1) * chunk, chunk)
+        hess_out[rows, 0, :] = mask_row * (out_buf[rows, :] + part_in[lev - core + h, 1] * s_before)
+    for k in range(1, 4):
+        d = lev ^ k
+        arrived(part_in.at[d, 0], part_recv.at[d])
+    for h in range(2):
+        rows = pl.ds(2 * h * chunk, chunk)
+        hess_out[rows, 0, :] = mask_row * (out_buf[rows, :] + (part_in[h, 0] + part_in[2 + h, 0]) * s_before)
+    for k in range(1, 4):
+        part(0, k).wait_send()
+    part(1, 1).wait_send()
 
 
 def per_device(
@@ -455,7 +475,7 @@
     vmem, dma = pltpu.VMEM, pltpu.SemaphoreType.DMA
     obs, hess = pl.pallas_call(
         functools.partial(kernel, nb, nl, total, 1.0 / (nb * total)),
-        out_shape=(jax.ShapeDtypeStruct((1, ny), F32), jax.ShapeDtypeStruct((nb, ny), F32)),
+        out_shape=(jax.ShapeDtypeStruct((1, ny), F32), jax.ShapeDtypeStruct((nb, 1, ny), F32)),
         in_specs=[pl.BlockSpec(memory_space=pl.ANY)] * 12,
         out_specs=(pl.BlockSpec(memory_space=pltpu.VMEM),) * 2,
         scratch_shapes=[
@@ -490,7 +510,7 @@
             vmem((nb, ny), F32),
             vmem((4, 3, chunk, ny), F32),
             vmem((4, chunk, ny), F32),
-            vmem((2, 2, chunk, ny), F32),
+            vmem((2, 4, chunk, ny), F32),
             vmem((4, 2, chunk, ny), F32),
             vmem((4, 1, ny), F32),
             vmem((4, 1, ny), F32),
@@ -500,7 +520,7 @@
             vmem((nb, ny), F32),
             dma((11,)), dma((nl,)),
             dma((4,)), dma((4,)), dma((4,)), dma((4,)), dma((2,)), dma((2,)),
-            dma((4,)), dma((4,)), dma((4,)), dma((4,)), dma((4,)), dma((4,)),
+            dma((4,)), dma((4,)), dma((4,)), dma((4,)), dma((8,)), dma((8,)),
             dma((8,)), dma((8,)), dma((4,)), dma((4,)), dma((8,)), dma((8,)), dma((4,)), dma((4,)),
             pltpu.SemaphoreType.REGULAR, pltpu.SemaphoreType.REGULAR, pltpu.SemaphoreType.REGULAR,
         ],
@@ -512,7 +532,7 @@
             level_factor[None], background, coag_rate, obs_weight[None], obs_precision,
         )
     ])
-    return obs, hess[:, None, :]
+    return obs, hess
 
 
 def solution(mesh):

time: 29.1 us -> 28.6 us (0.983)
  Pallas kernels: 27.1 us -> 26.6 us
    pallas_call x1, Pallas kernels: 27.1 us -> 26.6 us  [per_device(): pl.pallas_call(functools.partial(kernel, nb, nl, total, 1.0 / (nb * total...]
where the time goes in v4:
time: 28.6 us; the launch traced here: 28.5 us
  Pallas kernels  26.6 us (93%)
  local copies, waits for them, and re-layouts  1.2 us (4%)
  between operations  0.64 us (2%)
    pallas_call x1, Pallas kernels, per_device(): pl.pallas_call(functools.partial(kernel, nb, nl, total, 1.0 / (nb * total...  26.6 us
    unnamed x2, local copies, waits for them, and re-layouts  1.2 us

profile of v4, /device:TPU:1, one launch (start us, length us, event | category | flops | bytes accessed | tf_op | source)
XLA Modules:
  0.0 28.5 jit_solution(1416419768706023553)
XLA Ops:
  0.6 26.6 %hessian.1 = (f32[1,256]{1,0:T(1,128)S(1)}, f32[96,1,256]{2,1,0:T(1,128)S(1)}) custom-call(f32[96,1,256]{2,1,0:T(1,128)} %control.1, s32[1,256]{1,0:T(1,128)} %mask_in.1, f32[1,96]{1,0:T(1,128)} %bitcast.5, f32[1,16]{1,0:T(1,128)} %bitcast.6, f32[2,16,1,256]{3,2,1,0:T(1,128)} %courant.1, s32[2,16,1,256]{3,2,1,0:T(1,128)} %upwind.1, f32[1,96]{1,0:T(1,128)} %bitcast.7, ...), custom_call_target="tpu_custom_call" | custom-call | tf_op jit(solution)/shard_map/hessian/pallas_call | solution.py:476
  27.3 0.6 %copy.16 = f32[1,256]{1,0:T(1,128)} copy(f32[1,256]{1,0:T(1,128)S(1)} %get-tuple-element.4) | data formatting | bytes 2048
  27.8 0.6 %copy.17 = f32[96,1,256]{2,1,0:T(1,128)} copy(f32[96,1,256]{2,1,0:T(1,128)S(1)} %get-tuple-element.5) | data formatting | bytes 196608

commit v5 on v4

--- a/solution.py
+++ b/solution.py
@@ -248,20 +248,46 @@
             def _():
                 halo(d).start()
 
-    @pl.when(jnp.logical_not(is_last))
-    def _():
-        faces()
+    faces()
+
+    @pl.when(jnp.logical_not(is_first))
+    def _():
+        send_halos()
+
+    face_x, face_y = face[0], face[1]
+    next_y = pltpu.roll(face_y, ny - 1, 1)
+    coef[0] = jnp.maximum(face_y, 0.0)
+    coef[1] = -jnp.minimum(next_y, 0.0)
+    coef[2] = jnp.maximum(face_x, 0.0)
+    coef[3] = face[2] + jnp.minimum(face_x, 0.0) + jnp.minimum(face_y, 0.0) - jnp.maximum(next_y, 0.0)
+    for n in range(3):
+        quot[n] = dot3(chain, coef[n])
+        here[n] = coef[n, own, :]
+
+    def others(c, t_sum):
+        rows = rows_of(c)
+        sums = [jnp.zeros((chunk, ny), F32) for _ in range(3)]
+        for l in range(nl):
+            value = bfield[l, rows, :]
+            for n in range(3):
+                sums[n] = sums[n] + value * here[n, l:l + 1, :]
+        prof = wide(rb[nl, rows, :])
+        value = bfield[nl - 1, rows, :]
+        sums = [prof * (sums[n] + value * quot[n, rows, :]) for n in range(3)]
+        kern[c, 0] = sums[0]
+        kern[c, 1] = sums[1]
+        kern[c, 3] = sums[2]
+        part = masked[1, rows, :] * sums[0] + masked[2, rows, :] * sums[1]
+        for r in range(0, chunk, 8):
+            t_sum = t_sum + part[r:r + 8]
+        return t_sum
+
+    t_sum = lax.fori_loop(0, 4, others, jnp.zeros((8, ny), F32))
 
     @pl.when(is_first)
     def _():
         pl.semaphore_wait(near_sem, 2)
-
-    @pl.when(jnp.logical_not(is_last))
-    def _():
         send_halos()
-
-    @pl.when(is_first)
-    def _():
         edges[1].start()
         pl.semaphore_wait(far_sem, 2)
 
@@ -304,23 +330,10 @@
 
     lax.fori_loop(0, 4, next_row, 0)
 
-    @pl.when(is_last)
-    def _():
-        faces()
-        send_halos()
-
-    face_x, face_y = face[0], face[1]
-    next_y = pltpu.roll(face_y, ny - 1, 1)
-    coef[0] = jnp.maximum(face_y, 0.0)
-    coef[1] = -jnp.minimum(next_y, 0.0)
-    coef[2] = (
-        face[2] + jnp.minimum(face_x, 0.0) + jnp.minimum(face_y, 0.0) - jnp.maximum(next_y, 0.0)
-        - jnp.maximum(nface[...], 0.0)
-    )
-    coef[3] = jnp.maximum(face_x, 0.0)
-    for n in range(4):
-        quot[n] = dot3(chain, coef[n])
-        here[n] = coef[n, own, :]
+    own_coef = coef[3] - jnp.maximum(nface[...], 0.0)
+    coef[3] = own_coef
+    quot[3] = dot3(chain, own_coef)
+    here[3] = coef[3, own, :]
 
     def mine_to(c):
         return send(kern.at[c, pl.ds(0, 3)], mine_in.at[lev], mine_send.at[c], mine_recv.at[lev], c, tile)
@@ -328,29 +341,32 @@
     def left(c):
         return send(kern.at[c, 3], left_in.at[lev], left_send.at[c], left_recv.at[lev], c, before)
 
-    def others(c, t_sum):
+    def cell(c, t_sum):
         rows = rows_of(c)
-        sums = [jnp.zeros((chunk, ny), F32) for _ in range(4)]
+        total_here = jnp.zeros((chunk, ny), F32)
         for l in range(nl):
-            value = bfield[l, rows, :]
-            for n in range(4):
-                sums[n] = sums[n] + value * here[n, l:l + 1, :]
-        prof = wide(rb[nl, rows, :])
-        value = bfield[nl - 1, rows, :]
-        sums = [prof * (sums[n] + value * quot[n, rows, :]) for n in range(4)]
-        for n in range(4):
-            kern[c, n] = sums[n]
-
-        @pl.when(c != lev)
-        def _():
-            mine_to(c).start()
-        left(c).start()
-        part = masked[0, rows, :] * sums[2] + masked[1, rows, :] * sums[0] + masked[2, rows, :] * sums[1]
+            total_here = total_here + bfield[l, rows, :] * here[3, l:l + 1, :]
+        total_here = wide(rb[nl, rows, :]) * (total_here + bfield[nl - 1, rows, :] * quot[3, rows, :])
+        kern[c, 2] = total_here
+        part = masked[0, rows, :] * total_here
         for r in range(0, chunk, 8):
             t_sum = t_sum + part[r:r + 8]
         return t_sum
 
-    t_sum = lax.fori_loop(0, 4, others, jnp.zeros((8, ny), F32))
+    t_sum = lax.fori_loop(0, 4, cell, t_sum)
+
+    def send_sums():
+        for c in range(4):
+            @pl.when(c != lev)
+            def _():
+                mine_to(c).start()
+        for c in range(4):
+            left(c).start()
+
+    @pl.when(jnp.logical_not(is_last))
+    def _():
+        send_sums()
+
     for n in range(2):
         arrived(edge.at[n], edge_recv.at[n])
     for c in range(4):
@@ -363,14 +379,15 @@
     t_own[...] = t_mine
     s_own[...] = s_mine
 
-    t_sends = []
-    for k in range(4):
-        t_sends.append(send(s_own, t_left.at[lev], tx_send.at[k], tx_recv.at[lev], k, after))
-        t_sends.append(send(s_own, t_right.at[lev], tx_send.at[4 + k], tx_recv.at[4 + lev], k, before))
-    for k in range(1, 4):
-        t_sends.append(send(t_own, t_lev.at[k], tl_send.at[k], tl_recv.at[k], lev ^ k, tile))
+    t_sends = [send(s_own, t_left.at[lev], tx_send.at[k], tx_recv.at[lev], k, after) for k in range(4)]
+    t_sends += [send(t_own, t_lev.at[k], tl_send.at[k], tl_recv.at[k], lev ^ k, tile) for k in range(1, 4)]
+    t_sends += [send(s_own, t_right.at[lev], tx_send.at[4 + k], tx_recv.at[4 + lev], k, before) for k in range(4)]
     for copy in t_sends:
         copy.start()
+
+    @pl.when(is_last)
+    def _():
+        send_sums()
 
     def part(n, k):
         return send(
@@ -381,7 +398,7 @@
         for k in range(2):
             arrived(right_in.at[0, k], right_recv.at[k])
         part_in[lev, 0] = right_in[0, 0] + right_in[0, 1]
-        for k in range(1, 4):
+        for k in (2, 3, 1):
             part(0, k).start()
         for k in range(4):
             arrived(right_in.at[1, k], right_recv.at[4 + k])
@@ -443,26 +460,25 @@
     for copy in gathers:
         copy.wait_send()
 
+    for k in range(1, 4):
+        d = lev ^ k
+        arrived(out_buf.at[rows_of(d)], ag_recv.at[d])
+    arrived(part_in.at[lev ^ 1, 1], part_recv.at[4 + (lev ^ 1)])
+    for k in range(1, 4):
+        d = lev ^ k
+        arrived(part_in.at[d, 0], part_recv.at[d])
+    for k in range(1, 4):
+        part(0, k).wait_send()
+    part(1, 1).wait_send()
     for k in range(4):
         arrived(t_left.at[k], tx_recv.at[k])
     s_before = (t_left[0] + t_left[1]) + (t_left[2] + t_left[3])
-    for k in range(1, 4):
-        d = lev ^ k
-        arrived(out_buf.at[rows_of(d)], ag_recv.at[d])
     mask_row = mask[...].astype(F32)
-    arrived(part_in.at[lev ^ 1, 1], part_recv.at[4 + (lev ^ 1)])
     for h in range(2):
         rows = pl.ds((2 * h + 1) * chunk, chunk)
         hess_out[rows, 0, :] = mask_row * (out_buf[rows, :] + part_in[lev - core + h, 1] * s_before)
-    for k in range(1, 4):
-        d = lev ^ k
-        arrived(part_in.at[d, 0], part_recv.at[d])
-    for h in range(2):
         rows = pl.ds(2 * h * chunk, chunk)
         hess_out[rows, 0, :] = mask_row * (out_buf[rows, :] + (part_in[h, 0] + part_in[2 + h, 0]) * s_before)
-    for k in range(1, 4):
-        part(0, k).wait_send()
-    part(1, 1).wait_send()
 
 
 def per_device(

time: 28.6 us -> 28.6 us (level)
  no operation moved by 1% of the time
where the time goes in v5:
time: 28.6 us; the launch traced here: 28.5 us
  Pallas kernels  26.6 us (93%)
  local copies, waits for them, and re-layouts  1.2 us (4%)
  between operations  0.64 us (2%)
    pallas_call x1, Pallas kernels, per_device(): pl.pallas_call(functools.partial(kernel, nb, nl, total, 1.0 / (nb * total...  26.6 us
    unnamed x2, local copies, waits for them, and re-layouts  1.2 us

profile of v5, /device:TPU:1, one launch (start us, length us, event | category | flops | bytes accessed | tf_op | source)
XLA Modules:
  0.0 28.5 jit_solution(14294019008463713475)
XLA Ops:
  0.6 26.6 %hessian.1 = (f32[1,256]{1,0:T(1,128)S(1)}, f32[96,1,256]{2,1,0:T(1,128)S(1)}) custom-call(f32[96,1,256]{2,1,0:T(1,128)} %control.1, s32[1,256]{1,0:T(1,128)} %mask_in.1, f32[1,96]{1,0:T(1,128)} %bitcast.5, f32[1,16]{1,0:T(1,128)} %bitcast.6, f32[2,16,1,256]{3,2,1,0:T(1,128)} %courant.1, s32[2,16,1,256]{3,2,1,0:T(1,128)} %upwind.1, f32[1,96]{1,0:T(1,128)} %bitcast.7, ...), custom_call_target="tpu_custom_call" | custom-call | tf_op jit(solution)/shard_map/hessian/pallas_call | solution.py:492
  27.3 0.6 %copy.16 = f32[1,256]{1,0:T(1,128)} copy(f32[1,256]{1,0:T(1,128)S(1)} %get-tuple-element.4) | data formatting | bytes 2048
  27.8 0.6 %copy.17 = f32[96,1,256]{2,1,0:T(1,128)} copy(f32[96,1,256]{2,1,0:T(1,128)S(1)} %get-tuple-element.5) | data formatting | bytes 196608

commit v6 on v5

--- a/solution.py
+++ b/solution.py
@@ -379,7 +379,10 @@
     t_own[...] = t_mine
     s_own[...] = s_mine
 
-    t_sends = [send(s_own, t_left.at[lev], tx_send.at[k], tx_recv.at[lev], k, after) for k in range(4)]
+    t_sends = [
+        send(s_own, t_left.at[lev], tx_send.at[k], tx_recv.at[lev], 2 - lev_after + core + k if k < 2 else lev_after - core + k - 2, after)
+        for k in range(4)
+    ]
     t_sends += [send(t_own, t_lev.at[k], tl_send.at[k], tl_recv.at[k], lev ^ k, tile) for k in range(1, 4)]
     t_sends += [send(s_own, t_right.at[lev], tx_send.at[4 + k], tx_recv.at[4 + lev], k, before) for k in range(4)]
     for copy in t_sends:
@@ -464,11 +467,6 @@
         d = lev ^ k
         arrived(out_buf.at[rows_of(d)], ag_recv.at[d])
     arrived(part_in.at[lev ^ 1, 1], part_recv.at[4 + (lev ^ 1)])
-    for k in range(1, 4):
-        d = lev ^ k
-        arrived(part_in.at[d, 0], part_recv.at[d])
-    for k in range(1, 4):
-        part(0, k).wait_send()
     part(1, 1).wait_send()
     for k in range(4):
         arrived(t_left.at[k], tx_recv.at[k])
@@ -477,6 +475,12 @@
     for h in range(2):
         rows = pl.ds((2 * h + 1) * chunk, chunk)
         hess_out[rows, 0, :] = mask_row * (out_buf[rows, :] + part_in[lev - core + h, 1] * s_before)
+    for k in range(1, 4):
+        part(0, k).wait_send()
+    for k in range(1, 4):
+        d = lev ^ k
+        arrived(part_in.at[d, 0], part_recv.at[d])
+    for h in range(2):
         rows = pl.ds(2 * h * chunk, chunk)
         hess_out[rows, 0, :] = mask_row * (out_buf[rows, :] + (part_in[h, 0] + part_in[2 + h, 0]) * s_before)
 

time: 28.6 us -> 28.6 us (level)
  no operation moved by 1% of the time
where the time goes in v6:
time: 28.6 us; the launch traced here: 28.5 us
  Pallas kernels  26.6 us (93%)
  local copies, waits for them, and re-layouts  1.2 us (4%)
  between operations  0.64 us (2%)
    pallas_call x1, Pallas kernels, per_device(): pl.pallas_call(functools.partial(kernel, nb, nl, total, 1.0 / (nb * total...  26.6 us
    unnamed x2, local copies, waits for them, and re-layouts  1.2 us

profile of v6, /device:TPU:1, one launch (start us, length us, event | category | flops | bytes accessed | tf_op | source)
XLA Modules:
  0.0 28.5 jit_solution(251790452359675286)
XLA Ops:
  0.6 26.6 %hessian.1 = (f32[1,256]{1,0:T(1,128)S(1)}, f32[96,1,256]{2,1,0:T(1,128)S(1)}) custom-call(f32[96,1,256]{2,1,0:T(1,128)} %control.1, s32[1,256]{1,0:T(1,128)} %mask_in.1, f32[1,96]{1,0:T(1,128)} %bitcast.5, f32[1,16]{1,0:T(1,128)} %bitcast.6, f32[2,16,1,256]{3,2,1,0:T(1,128)} %courant.1, s32[2,16,1,256]{3,2,1,0:T(1,128)} %upwind.1, f32[1,96]{1,0:T(1,128)} %bitcast.7, ...), custom_call_target="tpu_custom_call" | custom-call | tf_op jit(solution)/shard_map/hessian/pallas_call | solution.py:496
  27.3 0.6 %copy.16 = f32[1,256]{1,0:T(1,128)} copy(f32[1,256]{1,0:T(1,128)S(1)} %get-tuple-element.4) | data formatting | bytes 2048
  27.9 0.6 %copy.17 = f32[96,1,256]{2,1,0:T(1,128)} copy(f32[96,1,256]{2,1,0:T(1,128)S(1)} %get-tuple-element.5) | data formatting | bytes 196608

commit v7 on v5

--- a/solution.py
+++ b/solution.py
@@ -288,8 +288,8 @@
     def _():
         pl.semaphore_wait(near_sem, 2)
         send_halos()
+        pl.semaphore_wait(far_sem, 2)
         edges[1].start()
-        pl.semaphore_wait(far_sem, 2)
 
     for d in range(4):
         @pl.when(d == lev)

time: 28.6 us -> 28.6 us (level)
  no operation moved by 1% of the time
where the time goes in v7:
time: 28.6 us; the launch traced here: 28.5 us
  Pallas kernels  26.6 us (93%)
  local copies, waits for them, and re-layouts  1.2 us (4%)
  between operations  0.64 us (2%)
    pallas_call x1, Pallas kernels, per_device(): pl.pallas_call(functools.partial(kernel, nb, nl, total, 1.0 / (nb * total...  26.6 us
    unnamed x2, local copies, waits for them, and re-layouts  1.2 us

profile of v7, /device:TPU:1, one launch (start us, length us, event | category | flops | bytes accessed | tf_op | source)
XLA Modules:
  0.0 28.5 jit_solution(7784851784388670355)
XLA Ops:
  0.6 26.6 %hessian.1 = (f32[1,256]{1,0:T(1,128)S(1)}, f32[96,1,256]{2,1,0:T(1,128)S(1)}) custom-call(f32[96,1,256]{2,1,0:T(1,128)} %control.1, s32[1,256]{1,0:T(1,128)} %mask_in.1, f32[1,96]{1,0:T(1,128)} %bitcast.5, f32[1,16]{1,0:T(1,128)} %bitcast.6, f32[2,16,1,256]{3,2,1,0:T(1,128)} %courant.1, s32[2,16,1,256]{3,2,1,0:T(1,128)} %upwind.1, f32[1,96]{1,0:T(1,128)} %bitcast.7, ...), custom_call_target="tpu_custom_call" | custom-call | tf_op jit(solution)/shard_map/hessian/pallas_call | solution.py:492
  27.3 0.6 %copy.16 = f32[1,256]{1,0:T(1,128)} copy(f32[1,256]{1,0:T(1,128)S(1)} %get-tuple-element.4) | data formatting | bytes 2048
  27.8 0.6 %copy.17 = f32[96,1,256]{2,1,0:T(1,128)} copy(f32[96,1,256]{2,1,0:T(1,128)S(1)} %get-tuple-element.5) | data formatting | bytes 196608
